TPU v7x, 32 devices: a whole 2x2x4 slice. The times are simulated.
32 devices in a mesh: hours: 2 (over x), chan: 2 (over core), freq: 8 (over z, y).
Axes of the slice: x: 2, y: 2, z: 4, core: 2. Of those that a mesh axis runs over, the one named last changes fastest.
Arguments:
- samples: bfloat16 [1152, 32, 1024], P('chan', ('hours', 'freq')), parts along dimension 1, may hold values from -18 to 18
Outputs:
- cross_spectra: bfloat16 [2, 256, 1152, 1152], P(None, ('hours', 'freq'), None, 'chan'), parts along dimension 1
There are 2 independent parts, one for each index of `hours`. A program takes and returns all parts, laid end to end along the dimension named above; each array names one. Nothing has to cross between parts.
All inputs are finite; a program needn't handle non-finite values.
Results may differ from a plain program's by a relative error of at most 0.008.
Values may be sent and summed in bfloat16 or wider, within the bound.
A program may use at most 192 MiB of HBM per device.

v0:
```python
import math

import jax
import jax.numpy as jnp
from jax import lax
from jax.sharding import PartitionSpec as P

BINS = 128


def padded_2(cells, sides, width):
    for axis, dim in sides:
        count = lax.axis_size(axis)
        ends = count - 1
        head = lax.slice_in_dim(cells, 0, width, axis=dim)
        tail = lax.slice_in_dim(cells, cells.shape[dim] - width, cells.shape[dim], axis=dim)
        cells = jnp.concatenate(
            [
                lax.ppermute(tail, axis, [(i, (i + 1) % count) for i in range(ends)]),
                cells,
                lax.ppermute(head, axis, [((i + 1) % count, i) for i in range(ends)]),
            ],
            axis=dim,
        )
    return cells


def from_behind(value, axis, steps):
    count = lax.axis_size(axis)
    pairs = [(source, (source + steps) % count) for source in range(count)]
    return lax.ppermute(value, axis, pairs)


def bin_table(length, bins):
    position = lax.broadcasted_iota(jnp.int32, (length, bins), 0)
    number = lax.broadcasted_iota(jnp.int32, (length, bins), 1) + 1
    phase = (position * number % length).astype(jnp.float32) * (2.0 * math.pi / length)
    taper = 0.5 - 0.5 * jnp.cos(position.astype(jnp.float32) * (2.0 * math.pi / length))
    factor = math.sqrt(8.0 / (3.0 * length))
    table = jnp.concatenate([taper * jnp.cos(phase), -(taper * jnp.sin(phase))], axis=1) * factor
    return table.astype(jnp.bfloat16)


def whiten(padded, first_bin, total_bins):
    count_bins = padded.shape[1] - 4
    values = padded.astype(jnp.float32)
    power = values[0] * values[0] + values[1] * values[1]
    summed = power[0:count_bins] + power[1 : count_bins + 1]
    summed = summed + power[2 : count_bins + 2]
    summed = summed + power[3 : count_bins + 3]
    summed = summed + power[4 : count_bins + 4]
    which = first_bin + jnp.arange(count_bins, dtype=jnp.int32)
    upper = jnp.minimum(which + 2, total_bins - 1)
    lower = jnp.maximum(which - 2, 0)
    count = (upper - lower + 1).astype(jnp.float32)
    level = jnp.maximum(summed / count[:, None, None], 0.1)
    return (values[:, 2 : count_bins + 2] / jnp.sqrt(level)[None]).astype(jnp.bfloat16)


def local(samples):
    local_channels, local_windows, length = samples.shape
    table = bin_table(length, BINS)
    spectrum = jnp.einsum("cws,sj->jwc", samples, table, preferred_element_type=jnp.float32)
    spectrum = spectrum.reshape(2, BINS, local_windows, local_channels).astype(jnp.bfloat16)
    arrived = lax.all_to_all(spectrum, "freq", split_axis=1, concat_axis=2, tiled=True)
    rimmed = padded_2(arrived, (("freq", 1),), 2)
    whitened = whiten(rimmed, lax.axis_index("freq") * arrived.shape[1], BINS)
    local_bins = whitened.shape[1]
    windows = whitened.shape[2]
    blocks = lax.axis_size("chan")
    own_block = lax.axis_index("chan")
    scale = 1.0 / windows
    visitors = [whitened]
    visiting = whitened
    visiting = from_behind(visiting, "chan", 1)
    visitors.append(visiting)
    stacked = jnp.stack(visitors)
    order = (own_block - jnp.arange(blocks, dtype=jnp.int32)) % blocks
    ordered = jnp.take(stacked, order, axis=0)
    every = jnp.transpose(ordered, (1, 2, 3, 0, 4)).reshape(
        2, local_bins, windows, blocks * local_channels
    )
    real_part = jnp.einsum("pkwb,pkwa->kba", every, whitened, preferred_element_type=jnp.float32)
    imag_part = jnp.einsum(
        "kwb,kwa->kba", every[0], whitened[1], preferred_element_type=jnp.float32
    )
    imag_part = imag_part - jnp.einsum(
        "kwb,kwa->kba", every[1], whitened[0], preferred_element_type=jnp.float32
    )
    return (jnp.stack([real_part, imag_part]) * scale).astype(jnp.bfloat16)


def solution(mesh):
    placed = (P("chan", ("hours", "freq"), None),)
    return jax.shard_map(
        local,
        mesh=mesh,
        in_specs=placed,
        out_specs=P(None, ("hours", "freq"), None, "chan"),
        check_vma=False,
    )
```

profile of v0, /device:TPU:15, one launch (start us, length us, event | category | flops | bytes accessed | tf_op | source)
XLA Modules:
  0.0 165.4 jit_solution(10404083622506896489)
XLA Ops:
  0.1 2.1 %cosine_multiply_fusion = (f32[1024,128]{1,0:T(8,128)S(1)}, f32[1024,128]{1,0:T(8,128)S(1)}) fusion(s32[128]{0:T(128)S(1)} %iota_add_fusion, f32[1024]{0:T(1024)S(1)} %multiply_subtract_fusion), kind=kLoop, calls=%fused_computation.36 | loop fusion | flops 2228224 | bytes 1053184 | tf_op jit(solution)/shard_map/mul | solution.py:40
  2.2 0.8 fusion.7
  3.0 0.1 convert_element_type.44
  3.1 2.7 %copy.14 = bf16[2,128,2,576]{3,2,0,1:T(2,128)(2,1)} copy(bf16[2,128,2,576]{1,0,3,2:T(2,128)(2,1)S(1)} %convert_element_type.44) | data formatting | bytes 1179648 | tf_op jit(solution)/shard_map/convert_element_type | solution.py:64
  5.8 5.7 %all-to-all-start = ((bf16[2,128,2,576]{3,2,0,1:T(2,128)(2,1)}), bf16[2,128,2,576]{3,2,0,1:T(2,128)(2,1)S(1)}, u32[]{:S(2)}, u32[]{:S(2)}) async-start(bf16[2,128,2,576]{3,2,0,1:T(2,128)(2,1)} %copy.14), calls=%async_computation | async-start | bytes 1310720 | tf_op jit(solution)/shard_map/all_to_all | solution.py:65
  11.5 14.8 %all-to-all-done = bf16[2,128,2,576]{3,2,0,1:T(2,128)(2,1)S(1)} async-done(((bf16[2,128,2,576]{3,2,0,1:T(2,128)(2,1)}), bf16[2,128,2,576]{3,2,0,1:T(2,128)(2,1)S(1)}, u32[]{:S(2)}, u32[]{:S(2)}) %all-to-all-start) | async-done | bytes 589856 | tf_op jit(solution)/shard_map/all_to_all | solution.py:65
  26.3 0.7 copy.16
  27.0 0.5 all_to_all.16
  27.5 3.1 %collective-permute-start = (bf16[2,2,16,576]{3,2,1,0:T(8,128)(2,1)S(1)}, bf16[2,2,16,576]{3,2,1,0:T(8,128)(2,1)S(1)}, u32[]{:S(2)}, u32[]{:S(2)}) collective-permute-start(bf16[2,2,16,576]{3,2,1,0:T(8,128)(2,1)S(1)} %get-tuple-element.7), channel_id=1, source_target_pairs={{0,1},{1,2},{2,3},{3,4},{4,5},{5,6},{6,7},{8,9},{9,10},{10,11},{11... | collective-permute-start | bytes 221192 | tf_op jit(solution)/shard_map/ppermute | solution.py:19
  30.7 2.1 %collective-permute-start.1 = (bf16[2,2,16,576]{3,2,1,0:T(8,128)(2,1)S(1)}, bf16[2,2,16,576]{3,2,1,0:T(8,128)(2,1)S(1)}, u32[]{:S(2)}, u32[]{:S(2)}) collective-permute-start(bf16[2,2,16,576]{3,2,1,0:T(8,128)(2,1)S(1)} %get-tuple-element.8), channel_id=1, source_target_pairs={{1,0},{2,1},{3,2},{4,3},{5,4},{6,5},{7,6},{9,8},{10,9},{11,10},{12... | collective-permute-start | bytes 221192 | tf_op jit(solution)/shard_map/ppermute | solution.py:21
  32.9 3.9 %collective-permute-done.1 = bf16[2,2,16,576]{3,2,1,0:T(8,128)(2,1)S(1)} collective-permute-done((bf16[2,2,16,576]{3,2,1,0:T(8,128)(2,1)S(1)}, bf16[2,2,16,576]{3,2,1,0:T(8,128)(2,1)S(1)}, u32[]{:S(2)}, u32[]{:S(2)}) %collective-permute-start.1) | collective-permute-done | bytes 73760 | tf_op jit(solution)/shard_map/ppermute | solution.py:21
  36.8 0.2 maximum_convert_fusion
  36.9 0.1 fusion.11
  37.0 0.3 fusion.15
  37.4 0.1 fusion.6
  37.5 2.1 %collective-permute-start.2 = (bf16[2,16,16,576]{3,2,1,0:T(8,128)(2,1)S(1)}, bf16[2,16,16,576]{3,2,1,0:T(8,128)(2,1)S(1)}, u32[]{:S(2)}, u32[]{:S(2)}) collective-permute-start(bf16[2,16,16,576]{3,2,1,0:T(8,128)(2,1)S(1)} %fusion.6), channel_id=1, source_target_pairs={{0,8},{8,0},{1,9},{9,1},{2,10},{10,2},{3,11},{11,3},{4,12},{12,4},... | collective-permute-start | bytes 1769480 | tf_op jit(solution)/shard_map/ppermute | solution.py:31
  39.7 0.1 fusion.37
  39.8 1.5 collective-permute-done.2
  41.3 0.2 pad_maximum_fusion
  41.5 1.8 %gather_fusion = bf16[2,2,16,16,576]{4,3,2,1,0:T(8,128)(2,1)} fusion(bf16[2,2,16,16,576]{4,3,2,1,0:T(8,128)(2,1)S(1)} %pad_maximum_fusion, s32[1024]{0:T(1024)S(1)} %pad_clamp_fusion), kind=kCustom, calls=%fused_computation | custom fusion | bytes 2359304 | tf_op jit(solution)/shard_map/jit(_take)/gather | solution.py:79
  43.3 1.5 select_bitcast_fusion
  44.8 2.4 %copy.17 = bf16[2,16,16,2,576]{4,3,2,1,0:T(2,128)(2,1)} copy(bf16[2,16,16,2,576]{4,2,1,0,3:T(8,128)(2,1)S(1)} %select_bitcast_fusion) | data formatting | bytes 2359296 | tf_op jit(solution)/shard_map/jit(_take)/select_n | solution.py:79
  47.2 1.0 fusion.31
  48.2 3.1 %reshape.85 = bf16[2,16,16,1152]{3,2,1,0:T(8,128)(2,1)S(1)} reshape(bf16[2,16,16,2,576]{4,3,2,1,0:T(2,128)(2,1)} %copy.17) | data formatting | bytes 2359296 | tf_op jit(solution)/shard_map/reshape | solution.py:80
  51.2 1.5 copy.19
  52.8 2.0 %squeeze.18 = bf16[16,16,1152]{2,1,0:T(8,128)(2,1)S(1)} reshape(bf16[1,16,16,2,576]{4,3,2,1,0:T(2,128)(2,1)} %copy.19) | data formatting | bytes 1179648 | tf_op jit(solution)/shard_map/squeeze | solution.py:88
  54.8 2.6 %copy.18 = bf16[1,16,16,2,576]{4,3,2,1,0:T(2,128)(2,1)} copy(bf16[1,16,16,2,576]{4,2,1,0,3:T(8,128)(2,1)} %get-tuple-element.6) | data formatting | bytes 1179648 | tf_op jit(solution)/shard_map/slice | solution.py:85
  57.4 2.0 %squeeze.16 = bf16[16,16,1152]{2,1,0:T(8,128)(2,1)S(1)} reshape(bf16[1,16,16,2,576]{4,3,2,1,0:T(2,128)(2,1)} %copy.18) | data formatting | bytes 1179648 | tf_op jit(solution)/shard_map/squeeze | solution.py:85
  59.4 16.5 %convolution_bitcast_fusion = f32[1,16,1152,576]{2,3,1,0:T(8,128)} fusion(bf16[2,16,16,1152]{3,2,1,0:T(8,128)(2,1)S(1)} %reshape.85, bf16[2,16,16,576]{3,2,1,0:T(8,128)(2,1)S(1)} %fusion.6), kind=kOutput, calls=%fused_computation.4 | convolution fusion | flops 679477248 | bytes 44236800 | tf_op jit(solution)/shard_map/pkwb,pkwa->kba/dot_general | solution.py:83
  75.9 17.6 %fusion.25 = f32[16,1152,576]{1,2,0:T(8,128)} fusion(bf16[16,16,1152]{2,1,0:T(8,128)(2,1)S(1)} %squeeze.16, bf16[2,16,16,576]{3,2,1,0:T(8,128)(2,1)S(1)} %fusion.6), kind=kOutput, calls=%fused_computation.42 | convolution fusion | flops 339738624 | bytes 43384832 | tf_op jit(solution)/shard_map/kwb,kwa->kba/dot_general | solution.py:84
  93.5 30.7 %subtract_bitcast_fusion = f32[1,16,1152,576]{2,3,1,0:T(8,128)} fusion(f32[16,1152,576]{1,2,0:T(8,128)} %fusion.25, bf16[16,16,1152]{2,1,0:T(8,128)(2,1)S(1)} %squeeze.18, bf16[2,16,16,576]{3,2,1,0:T(8,128)(2,1)S(1)} %fusion.6), kind=kOutput, calls=%fused_computation.3 | convolution fusion | flops 350355456 | bytes 85852160 | tf_op jit(solution)/shard_map/kwb,kwa->kba/dot_general | solution.py:87
  124.2 41.0 %fusion = bf16[2,16,1152,576]{2,3,1,0:T(8,128)(2,1)} fusion(f32[1,16,1152,576]{2,3,1,0:T(8,128)} %subtract_bitcast_fusion, f32[1,16,1152,576]{2,3,1,0:T(8,128)} %convolution_bitcast_fusion), kind=kLoop, calls=%fused_computation.2 | loop fusion | flops 63700992 | bytes 127401984 | tf_op jit(solution)/shard_map/convert_element_type | solution.py:90
  (13 shorter events, 0.2 us)
Async XLA Ops:
  0.0 2.2 %copy-start = (bf16[576,2,1024]{2,1,0:T(2,128)(2,1)S(1)}, bf16[576,2,1024]{2,1,0:T(2,128)(2,1)}, u32[]{:S(2)}) copy-start(bf16[576,2,1024]{2,1,0:T(2,128)(2,1)} %param.1) | copy-start | bytes 7077892
  5.8 20.4 %all-to-all-start = ((bf16[2,128,2,576]{3,2,0,1:T(2,128)(2,1)}), bf16[2,128,2,576]{3,2,0,1:T(2,128)(2,1)S(1)}, u32[]{:S(2)}, u32[]{:S(2)}) async-start(bf16[2,128,2,576]{3,2,0,1:T(2,128)(2,1)} %copy.14), calls=%async_computation | async-start | bytes 1310720 | tf_op jit(solution)/shard_map/all_to_all | solution.py:65
  27.5 5.3 %collective-permute-start = (bf16[2,2,16,576]{3,2,1,0:T(8,128)(2,1)S(1)}, bf16[2,2,16,576]{3,2,1,0:T(8,128)(2,1)S(1)}, u32[]{:S(2)}, u32[]{:S(2)}) collective-permute-start(bf16[2,2,16,576]{3,2,1,0:T(8,128)(2,1)S(1)} %get-tuple-element.7), channel_id=1, source_target_pairs={{0,1},{1,2},{2,3},{3,4},{4,5},{5,6},{6,7},{8,9},{9,10},{10,11},{11... | collective-permute-start | bytes 221192 | tf_op jit(solution)/shard_map/ppermute | solution.py:19
  30.7 6.1 %collective-permute-start.1 = (bf16[2,2,16,576]{3,2,1,0:T(8,128)(2,1)S(1)}, bf16[2,2,16,576]{3,2,1,0:T(8,128)(2,1)S(1)}, u32[]{:S(2)}, u32[]{:S(2)}) collective-permute-start(bf16[2,2,16,576]{3,2,1,0:T(8,128)(2,1)S(1)} %get-tuple-element.8), channel_id=1, source_target_pairs={{1,0},{2,1},{3,2},{4,3},{5,4},{6,5},{7,6},{9,8},{10,9},{11,10},{12... | collective-permute-start | bytes 221192 | tf_op jit(solution)/shard_map/ppermute | solution.py:21
  37.5 3.8 %collective-permute-start.2 = (bf16[2,16,16,576]{3,2,1,0:T(8,128)(2,1)S(1)}, bf16[2,16,16,576]{3,2,1,0:T(8,128)(2,1)S(1)}, u32[]{:S(2)}, u32[]{:S(2)}) collective-permute-start(bf16[2,16,16,576]{3,2,1,0:T(8,128)(2,1)S(1)} %fusion.6), channel_id=1, source_target_pairs={{0,8},{8,0},{1,9},{9,1},{2,10},{10,2},{3,11},{11,3},{4,12},{12,4},... | collective-permute-start | bytes 1769480 | tf_op jit(solution)/shard_map/ppermute | solution.py:31
  124.2 41.0 %copy-start.1 = (bf16[576,2,1024]{2,1,0:T(2,128)(2,1)S(1)}, bf16[576,2,1024]{2,1,0:T(2,128)(2,1)}, u32[]{:S(2)}) copy-start(bf16[576,2,1024]{2,1,0:T(2,128)(2,1)} %param.1) | copy-start | bytes 7077892
where the time goes:
time: 169 us; the launch traced here: 165 us
  matrix products  65.5 us (39%)
  other arithmetic  45.8 us (27%)
  local copies, waits for them, and re-layouts  20.4 us (12%)
  waiting for transfers between devices  20.2 us (12%)
  starting transfers between devices  13 us (8%)
    convert_element_type x1, other arithmetic, local(): return (jnp.stack([real_part, imag_part]) * scale).astype(jnp.bfloat16)  41 us
    dot_general x1, matrix products, local(): jnp.einsum('kwb,kwa->kba', every[1], whitened[0], preferred_element_type=...  30.7 us
    dot_general x1, matrix products, local(): jnp.einsum('kwb,kwa->kba', every[0], whitened[1], preferred_element_type=...  17.6 us
    dot_general x1, matrix products, local(): jnp.einsum('pkwb,pkwa->kba', every, whitened, preferred_element_type=jnp....  16.5 us
    all_to_all x1, waiting for transfers between devices, local(): lax.all_to_all(spectrum, 'freq', split_axis=1, concat_axis=2, tiled=True)  14.8 us
    all_to_all x1, starting transfers between devices, local(): lax.all_to_all(spectrum, 'freq', split_axis=1, concat_axis=2, tiled=True)  5.66 us
    ppermute x1, waiting for transfers between devices, padded_2(): lax.ppermute(head, axis, [((i + 1) % count, i) for i in range(ends)])  3.91 us
  transfers between devices with their start and end apart: 4, of which 3 were waited for; matrix products, arithmetic and copies ran while one was open for 0% of the time, Pallas kernels for 0%

commit v1 on v0

v1 whole, which is shorter than its diff:
```python
import functools
import math

import jax
import jax.numpy as jnp
import numpy as np
from jax import lax
from jax.experimental import pallas as pl
from jax.experimental.pallas import tpu as pltpu
from jax.sharding import PartitionSpec as P

BINS = 128
LANES = 128
MESH = pl.DeviceIdType.MESH


def bin_table(length, bins):
    position = np.arange(length, dtype=np.int64)[:, None]
    number = np.arange(bins, dtype=np.int64)[None, :] + 1
    step = np.float32(2.0 * math.pi / length)
    phase = (position * number % length).astype(np.float32) * step
    half = np.float32(0.5)
    taper = half - half * np.cos(position.astype(np.float32) * step)
    factor = np.float32(math.sqrt(8.0 / (3.0 * length)))
    table = np.concatenate([taper * np.cos(phase), -(taper * np.sin(phase))], axis=1) * factor
    return jnp.asarray(table.astype(np.float32)).astype(jnp.bfloat16)


def whiten(real, imag):
    bins = real.shape[0]
    power = real * real + imag * imag
    row = lax.broadcasted_iota(jnp.int32, (bins, 1), 0)
    summed = power
    for shift in (1, 2):
        summed = summed + jnp.where(row >= shift, pltpu.roll(power, shift, 0), 0.0)
        summed = summed + jnp.where(row < bins - shift, pltpu.roll(power, bins - shift, 0), 0.0)
    count = jnp.minimum(row + 2, bins - 1) - jnp.maximum(row - 2, 0) + 1
    level = jnp.maximum(summed * (1.0 / count.astype(jnp.float32)), 0.1)
    scale = lax.rsqrt(level)
    return (real * scale).astype(jnp.bfloat16), (imag * scale).astype(jnp.bfloat16)


def exchange_kernel(count, spec_ref, own_ref, other_ref, white, send_sem, recv_sem, local_sem,
                    pass_sem, got_sem):
    hour = lax.axis_index("hours")
    chan = lax.axis_index("chan")
    me = lax.axis_index("freq")
    windows, _, _ = spec_ref.shape
    local_bins = own_ref.shape[2]
    peers = [lax.rem(me + step, count) for step in range(1, count)]

    barrier = pltpu.get_barrier_semaphore()
    for peer in peers:
        pl.semaphore_signal(barrier, inc=1, device_id=(hour, chan, peer), device_id_type=MESH)
    pl.semaphore_signal(barrier, inc=1, device_id=(hour, 1 - chan, me), device_id_type=MESH)

    for w in range(windows):
        turned = spec_ref[w].astype(jnp.float32).T
        real, imag = whiten(turned[:BINS], turned[BINS:])
        white[0, w] = real.reshape(count, local_bins, real.shape[1])
        white[1, w] = imag.reshape(count, local_bins, imag.shape[1])

    pl.semaphore_wait(barrier, count)

    mine = pl.ds(windows * me, windows)
    copies = []
    for step in range(1, count):
        copy = pltpu.make_async_remote_copy(
            src_ref=white.at[:, :, peers[step - 1]],
            dst_ref=own_ref.at[:, mine],
            send_sem=send_sem.at[step],
            recv_sem=recv_sem.at[step],
            device_id=(hour, chan, peers[step - 1]),
            device_id_type=MESH,
        )
        copy.start()
        copies.append(copy)
    keep = pltpu.make_async_copy(white.at[:, :, me], own_ref.at[:, mine], local_sem)
    keep.start()
    passes = []

    def forward(source_ref, owner, slot):
        part = pl.ds(windows * owner, windows)
        copy = pltpu.make_async_remote_copy(
            src_ref=source_ref,
            dst_ref=other_ref.at[:, part],
            send_sem=pass_sem.at[slot],
            recv_sem=got_sem.at[slot],
            device_id=(hour, 1 - chan, me),
            device_id_type=MESH,
        )
        copy.start()
        passes.append(copy)

    forward(white.at[:, :, me], me, 0)
    for step in range(1, count):
        copies[step - 1].wait_recv()
        owner = lax.rem(me - step + count, count)
        forward(own_ref.at[:, pl.ds(windows * owner, windows)], owner, step)
    keep.wait()
    for copy in copies:
        copy.wait_send()
    for copy in passes:
        copy.wait()


def exchange(spec, count):
    windows, channels, _ = spec.shape
    local_bins = BINS // count
    shape = jax.ShapeDtypeStruct((2, windows * count, local_bins, channels), jnp.bfloat16)
    size = spec.size * 2
    return pl.pallas_call(
        functools.partial(exchange_kernel, count),
        out_shape=(shape, shape),
        in_specs=[pl.BlockSpec(memory_space=pltpu.VMEM)],
        out_specs=(pl.BlockSpec(memory_space=pl.ANY), pl.BlockSpec(memory_space=pl.ANY)),
        scratch_shapes=[
            pltpu.VMEM((2, windows, count, local_bins, channels), jnp.bfloat16),
            pltpu.SemaphoreType.DMA((count,)),
            pltpu.SemaphoreType.DMA((count,)),
            pltpu.SemaphoreType.DMA,
            pltpu.SemaphoreType.DMA((count,)),
            pltpu.SemaphoreType.DMA((count,)),
        ],
        compiler_params=pltpu.CompilerParams(
            collective_id=0, has_side_effects=True, vmem_limit_bytes=40 << 20
        ),
        cost_estimate=pl.CostEstimate(flops=spec.size * 20, bytes_accessed=size * 4, transcendentals=0),
        name="exchange",
    )(spec)


def spread(tiles, values):
    width = values.shape[1]
    for t in range(tiles.shape[0]):
        part = values[:, t * LANES : min((t + 1) * LANES, width)]
        if part.shape[1] < LANES:
            part = jnp.concatenate(
                [part, jnp.zeros((part.shape[0], LANES - part.shape[1]), part.dtype)], axis=1
            )
        tiles[t] = part


def cross_kernel(scale, own_ref, other_ref, out_ref, mine, every):
    chan = lax.axis_index("chan")
    parts, windows, local_bins, channels = own_ref.shape
    rows = parts * windows * local_bins
    k = pl.program_id(0)

    @pl.when(k == 0)
    def _():
        own = own_ref[...].astype(jnp.float32).reshape(rows, channels)
        other = other_ref[...].astype(jnp.float32).reshape(rows, channels)
        spread(mine, own)
        first = jnp.where(chan == 0, own, other)
        second = jnp.where(chan == 0, other, own)
        spread(every, jnp.concatenate([first, second], axis=1))

    pick = pl.ds(k, parts * windows, stride=local_bins)
    here = jnp.concatenate([mine[t, pick, :] for t in range(mine.shape[0])], axis=1)[:, :channels]
    left = here.astype(jnp.bfloat16)
    swapped = jnp.concatenate([here[windows:], -here[:windows]], axis=0).astype(jnp.bfloat16)
    right = jnp.concatenate(
        [every[t, pick, :].astype(jnp.bfloat16) for t in range(every.shape[0])], axis=1
    )[:, : 2 * channels]
    for part, side in ((0, left), (1, swapped)):
        product = lax.dot_general(
            side, right, (((0,), (0,)), ((), ())), preferred_element_type=jnp.float32
        )
        out_ref[part, 0] = (product * scale).astype(jnp.bfloat16)


def cross(own, other):
    parts, windows, local_bins, channels = own.shape
    rows = parts * windows * local_bins
    shape = (parts, local_bins, channels, 2 * channels)
    whole = pl.BlockSpec(memory_space=pltpu.VMEM)
    return pl.pallas_call(
        functools.partial(cross_kernel, 1.0 / windows),
        grid=(local_bins,),
        out_shape=jax.ShapeDtypeStruct(shape, jnp.bfloat16),
        in_specs=[whole, whole],
        out_specs=pl.BlockSpec((parts, 1, channels, 2 * channels), lambda k: (0, k, 0, 0)),
        scratch_shapes=[
            pltpu.VMEM((pl.cdiv(channels, LANES), rows, LANES), jnp.float32),
            pltpu.VMEM((pl.cdiv(2 * channels, LANES), rows, LANES), jnp.float32),
        ],
        compiler_params=pltpu.CompilerParams(vmem_limit_bytes=50 << 20),
        cost_estimate=pl.CostEstimate(
            flops=2 * rows * channels * 2 * channels * 2,
            bytes_accessed=2 * math.prod(shape),
            transcendentals=0,
        ),
        name="cross",
    )(own, other)


def local(samples):
    length = samples.shape[2]
    table = bin_table(length, BINS)
    spec = jnp.einsum("cws,sj->wcj", samples, table, preferred_element_type=jnp.float32)
    own, other = exchange(spec.astype(jnp.bfloat16), lax.axis_size("freq"))
    return jnp.swapaxes(cross(own, other), 2, 3)


def solution(mesh):
    return jax.shard_map(
        local,
        mesh=mesh,
        in_specs=(P("chan", ("hours", "freq"), None),),
        out_specs=P(None, ("hours", "freq"), None, "chan"),
        check_vma=False,
    )
```

time: 169 us -> 44.7 us (0.26); the launches traced: 165 us -> 44.5 us
  matrix products: 65.5 us -> 1.83 us
  other arithmetic: 45.8 us -> 0 us
  Pallas kernels: 0 us -> 41 us
  waiting for transfers between devices: 20.2 us -> 0 us
  local copies, waits for them, and re-layouts: 20.4 us -> 1.67 us
  starting transfers between devices: 13 us -> 0 us
    dot_general x4 -> x1, matrix products: 65.5 us -> 1.83 us  [local(): jnp.einsum('cws,sj->wcj', samples, table, preferred_element_type=jnp.floa...]
    convert_element_type x4 -> x0, other arithmetic: 41.3 us -> none  [the longest x1 41 us: local(): return (jnp.stack([real_part, imag_part]) * scale).astype(jnp.bfloat16)]
    pallas_call x0 -> x2, Pallas kernels: none -> 41 us  [the longest x1 20.7 us: cross(): pl.pallas_call(functools.partial(cross_kernel, 1.0 / windows), grid=(loca...]
    all_to_all x1 -> x0, waiting for transfers between devices: 14.8 us -> none  [local(): lax.all_to_all(spectrum, 'freq', split_axis=1, concat_axis=2, tiled=True)]
    ppermute x3 -> x0, starting transfers between devices: 7.36 us -> none  [the longest x1 3.15 us: padded_2(): lax.ppermute(tail, axis, [(i, (i + 1) % count) for i in range(ends)])]
    all_to_all x1 -> x0, starting transfers between devices: 5.66 us -> none  [local(): lax.all_to_all(spectrum, 'freq', split_axis=1, concat_axis=2, tiled=True)]
    ppermute x3 -> x0, waiting for transfers between devices: 5.44 us -> none  [the longest x1 3.91 us: padded_2(): lax.ppermute(head, axis, [((i + 1) % count, i) for i in range(ends)])]
    slice x4 -> x0, local copies, waits for them, and re-layouts: 5.08 us -> none  [the longest x1 2.6 us: local(): every[0]]
  transfers between devices with their start and end apart: 4 -> 0, of which waited for: 3 -> 0; matrix products, arithmetic and copies ran while one was open for 0% -> 0% of each run, Pallas kernels for 0% -> 0%
where the time goes in v1:
time: 44.7 us; the launch traced here: 44.5 us
  Pallas kernels  41 us (92%)
  matrix products  1.83 us (4%)
  local copies, waits for them, and re-layouts  1.67 us (4%)
    pallas_call x1, Pallas kernels, cross(): pl.pallas_call(functools.partial(cross_kernel, 1.0 / windows), grid=(loca...  20.7 us
    pallas_call x1, Pallas kernels, exchange(): pl.pallas_call(functools.partial(exchange_kernel, count), out_shape=(shap...  20.4 us
    dot_general x1, matrix products, local(): jnp.einsum('cws,sj->wcj', samples, table, preferred_element_type=jnp.floa...  1.83 us
    unnamed x2, local copies, waits for them, and re-layouts  1.67 us

profile of v1, /device:TPU:15, one launch (start us, length us, event | category | flops | bytes accessed | tf_op | source)
XLA Modules:
  0.0 44.5 jit_solution(12107193435918350125)
XLA Ops:
  0.0 0.0 copy-start
  0.0 1.7 %copy-done = bf16[576,2,1024]{2,1,0:T(2,128)(2,1)S(1)} copy-done((bf16[576,2,1024]{2,1,0:T(2,128)(2,1)S(1)}, bf16[576,2,1024]{2,1,0:T(2,128)(2,1)}, u32[]{:S(2)}) %copy-start) | copy-done | bytes 2359320
  1.7 1.8 %fusion.5.spec_ref = bf16[2,576,256]{2,1,0:T(8,128)(2,1)S(1)} fusion(bf16[1024,256,1]{1,0,2:T(8,128)(2,1)} %constant.5, bf16[576,2,1024]{2,1,0:T(2,128)(2,1)S(1)} %copy-done), kind=kOutput, calls=%fused_computation.3 | convolution fusion | flops 604274688 | bytes 3473408 | tf_op jit(solution)/shard_map/cws,sj->wcj/dot_general | solution.py:201
  3.5 20.4 %exchange.1 = (bf16[2,16,16,576]{3,2,1,0:T(8,128)(2,1)S(1)}, bf16[2,16,16,576]{3,2,1,0:T(8,128)(2,1)S(1)}) custom-call(bf16[2,576,256]{2,1,0:T(8,128)(2,1)S(1)} %fusion.5.spec_ref), custom_call_target="tpu_custom_call" | custom-call | flops 5898240 | bytes 2359296 | tf_op jit(solution)/shard_map/exchange/pallas_call | solution.py:112
  23.9 20.7 %cross.1 = bf16[2,16,576,1152]{3,2,1,0:T(8,128)(2,1)} custom-call(bf16[2,16,16,576]{3,2,1,0:T(8,128)(2,1)S(1)} %get-tuple-element.7.own_ref, bf16[2,16,16,576]{3,2,1,0:T(8,128)(2,1)S(1)} %get-tuple-element.8.other_ref), custom_call_target="tpu_custom_call" | custom-call | flops 1358954496 | bytes 42467328 | tf_op jit(solution)/shard_map/cross/pallas_call | solution.py:178
Async XLA Ops:
  0.0 1.7 %copy-start = (bf16[576,2,1024]{2,1,0:T(2,128)(2,1)S(1)}, bf16[576,2,1024]{2,1,0:T(2,128)(2,1)}, u32[]{:S(2)}) copy-start(bf16[576,2,1024]{2,1,0:T(2,128)(2,1)} %param.2) | copy-start | bytes 7077892

commit v2 on v1

v2 whole, which is shorter than its diff:
```python
import functools
import math

import jax
import jax.numpy as jnp
import numpy as np
from jax import lax
from jax.experimental import pallas as pl
from jax.experimental.pallas import tpu as pltpu
from jax.sharding import PartitionSpec as P

BINS = 128
LANES = 128
MESH = pl.DeviceIdType.MESH


def bin_table(length, bins):
    position = np.arange(length, dtype=np.int64)[:, None]
    number = np.arange(bins, dtype=np.int64)[None, :] + 1
    step = np.float32(2.0 * math.pi / length)
    phase = (position * number % length).astype(np.float32) * step
    half = np.float32(0.5)
    taper = half - half * np.cos(position.astype(np.float32) * step)
    factor = np.float32(math.sqrt(8.0 / (3.0 * length)))
    table = np.concatenate([taper * np.cos(phase), -(taper * np.sin(phase))], axis=1) * factor
    return jnp.asarray(table.astype(np.float32)).astype(jnp.bfloat16)


def whiten(real, imag):
    bins = real.shape[0]
    power = real * real + imag * imag
    row = lax.broadcasted_iota(jnp.int32, (bins, 1), 0)
    summed = power
    for shift in (1, 2):
        summed = summed + jnp.where(row >= shift, pltpu.roll(power, shift, 0), 0.0)
        summed = summed + jnp.where(row < bins - shift, pltpu.roll(power, bins - shift, 0), 0.0)
    count = jnp.minimum(row + 2, bins - 1) - jnp.maximum(row - 2, 0) + 1
    level = jnp.maximum(summed * (1.0 / count.astype(jnp.float32)), 0.1)
    scale = lax.rsqrt(level)
    return real * scale, imag * scale


def pack(real, imag):
    cut = real.shape[1] // LANES * LANES
    return jnp.concatenate([real[:, :cut], imag[:, :cut], real[:, cut:], imag[:, cut:]], axis=1)


def unpack(values, part, channels):
    cut = channels // LANES * LANES
    rest = channels - cut
    tail = 2 * cut + part * rest
    main = values[:, part * cut : (part + 1) * cut]
    return jnp.concatenate([main, values[:, tail : tail + rest]], axis=1) if rest else main


def exchange_kernel(count, spec_ref, own_ref, other_ref, white, send_sem, recv_sem, local_sem,
                    pass_sem, got_sem):
    hour = lax.axis_index("hours")
    chan = lax.axis_index("chan")
    me = lax.axis_index("freq")
    windows = spec_ref.shape[0]
    local_bins, width = own_ref.shape[1:]
    steps = sorted(range(1, count), key=lambda step: abs(2 * step - count))

    barrier = pltpu.get_barrier_semaphore()
    for step in steps:
        peer = lax.rem(me + step, count)
        pl.semaphore_signal(barrier, inc=1, device_id=(hour, chan, peer), device_id_type=MESH)
    pl.semaphore_signal(barrier, inc=1, device_id=(hour, 1 - chan, me), device_id_type=MESH)

    copies, keeps, passes = {}, [], []

    def forward(source_ref, owner, w, step):
        slot = w * count + step
        copy = pltpu.make_async_remote_copy(
            src_ref=source_ref,
            dst_ref=other_ref.at[windows * owner + w],
            send_sem=pass_sem.at[slot],
            recv_sem=got_sem.at[slot],
            device_id=(hour, 1 - chan, me),
            device_id_type=MESH,
        )
        copy.start()
        passes.append(copy)

    for w in range(windows):
        turned = spec_ref[w].astype(jnp.float32).T
        real, imag = whiten(turned[:BINS], turned[BINS:])
        packed = pack(real, imag).astype(jnp.bfloat16)
        white[w] = packed.reshape(count, local_bins, width)
        if w == 0:
            pl.semaphore_wait(barrier, count)
        for step in steps:
            peer = lax.rem(me + step, count)
            copy = pltpu.make_async_remote_copy(
                src_ref=white.at[w, peer],
                dst_ref=own_ref.at[windows * me + w],
                send_sem=send_sem.at[w * count + step],
                recv_sem=recv_sem.at[w * count + step],
                device_id=(hour, chan, peer),
                device_id_type=MESH,
            )
            copy.start()
            copies[w, step] = copy
    for w in range(windows):
        keep = pltpu.make_async_copy(white.at[w, me], own_ref.at[windows * me + w], local_sem.at[w])
        keep.start()
        keeps.append(keep)
        forward(white.at[w, me], me, w, 0)
    for w in range(windows):
        for step in reversed(steps):
            copies[w, step].wait_recv()
            owner = lax.rem(me - step + count, count)
            forward(own_ref.at[windows * owner + w], owner, w, step)
    for keep in keeps:
        keep.wait()
    for copy in copies.values():
        copy.wait_send()
    for copy in passes:
        copy.wait()


def exchange(spec, count):
    windows, channels, _ = spec.shape
    local_bins = BINS // count
    shape = jax.ShapeDtypeStruct((windows * count, local_bins, 2 * channels), jnp.bfloat16)
    pieces = pltpu.SemaphoreType.DMA((windows * count,))
    return pl.pallas_call(
        functools.partial(exchange_kernel, count),
        out_shape=(shape, shape),
        in_specs=[pl.BlockSpec(memory_space=pltpu.VMEM)],
        out_specs=(pl.BlockSpec(memory_space=pl.ANY), pl.BlockSpec(memory_space=pl.ANY)),
        scratch_shapes=[
            pltpu.VMEM((windows, count, local_bins, 2 * channels), jnp.bfloat16),
            pieces,
            pieces,
            pltpu.SemaphoreType.DMA((windows,)),
            pieces,
            pieces,
        ],
        compiler_params=pltpu.CompilerParams(
            collective_id=0, has_side_effects=True, vmem_limit_bytes=40 << 20
        ),
        cost_estimate=pl.CostEstimate(
            flops=spec.size * 20, bytes_accessed=spec.size * 8, transcendentals=0
        ),
        name="exchange",
    )(spec)


def spread(tiles, first_row, values):
    height, width = values.shape
    for t in range(tiles.shape[0]):
        part = values[:, t * LANES : min((t + 1) * LANES, width)]
        if part.shape[1] < LANES:
            gap = jnp.zeros((height, LANES - part.shape[1]), part.dtype)
            part = jnp.concatenate([part, gap], axis=1)
        tiles[t, first_row : first_row + height] = part


def cross_kernel(scale, own_ref, other_ref, out_ref, mine, every):
    chan = lax.axis_index("chan")
    windows, local_bins, width = own_ref.shape
    channels = width // 2
    rows = windows * local_bins
    step_bins = out_ref.shape[1]
    step = pl.program_id(0)

    @pl.when(step == 0)
    def _():
        own = own_ref[...].astype(jnp.float32).reshape(rows, width)
        other = other_ref[...].astype(jnp.float32).reshape(rows, width)
        first = jnp.where(chan == 0, own, other)
        second = jnp.where(chan == 0, other, own)
        for part in range(2):
            spread(mine, part * rows, unpack(own, part, channels))
            pair = [unpack(first, part, channels), unpack(second, part, channels)]
            spread(every, part * rows, jnp.concatenate(pair, axis=1))

    for b in range(step_bins):
        pick = pl.ds(step * step_bins + b, 2 * windows, stride=local_bins)
        here = [mine[t, pick, :] for t in range(mine.shape[0])]
        here = jnp.concatenate(here, axis=1)[:, :channels]
        left = here.astype(jnp.bfloat16)
        swapped = jnp.concatenate([here[windows:], -here[:windows]], axis=0).astype(jnp.bfloat16)
        right = [every[t, pick, :].astype(jnp.bfloat16) for t in range(every.shape[0])]
        right = jnp.concatenate(right, axis=1)[:, :width]
        for part, side in ((0, left), (1, swapped)):
            product = lax.dot_general(
                side, right, (((0,), (0,)), ((), ())), preferred_element_type=jnp.float32
            )
            out_ref[part, b] = (product * scale).astype(jnp.bfloat16)


def cross(own, other):
    windows, local_bins, width = own.shape
    channels = width // 2
    rows = 2 * windows * local_bins
    step_bins = 2 if local_bins % 2 == 0 else 1
    shape = (2, local_bins, channels, width)
    whole = pl.BlockSpec(memory_space=pltpu.VMEM)
    return pl.pallas_call(
        functools.partial(cross_kernel, 1.0 / windows),
        grid=(local_bins // step_bins,),
        out_shape=jax.ShapeDtypeStruct(shape, jnp.bfloat16),
        in_specs=[whole, whole],
        out_specs=pl.BlockSpec((2, step_bins, channels, width), lambda k: (0, k, 0, 0)),
        scratch_shapes=[
            pltpu.VMEM((pl.cdiv(channels, LANES), rows, LANES), jnp.float32),
            pltpu.VMEM((pl.cdiv(width, LANES), rows, LANES), jnp.float32),
        ],
        compiler_params=pltpu.CompilerParams(vmem_limit_bytes=50 << 20),
        cost_estimate=pl.CostEstimate(
            flops=2 * rows * channels * width * 2,
            bytes_accessed=2 * math.prod(shape),
            transcendentals=0,
        ),
        name="cross",
    )(own, other)


def local(samples):
    length = samples.shape[2]
    table = bin_table(length, BINS)
    spec = jnp.einsum("cws,sj->wcj", samples, table, preferred_element_type=jnp.float32)
    own, other = exchange(spec.astype(jnp.bfloat16), lax.axis_size("freq"))
    return jnp.swapaxes(cross(own, other), 2, 3)


def solution(mesh):
    return jax.shard_map(
        local,
        mesh=mesh,
        in_specs=(P("chan", ("hours", "freq"), None),),
        out_specs=P(None, ("hours", "freq"), None, "chan"),
        check_vma=False,
    )
```

time: 44.7 us -> 41.9 us (0.937)
  the two profiles are of different devices: /device:TPU:15 before, /device:TPU:0 now
where the time goes in v2:
time: 41.9 us; the launch traced here: 41.7 us
  Pallas kernels  38.2 us (91%)
  matrix products  1.83 us (4%)
  local copies, waits for them, and re-layouts  1.67 us (4%)
    pallas_call x1, Pallas kernels, exchange(): pl.pallas_call(functools.partial(exchange_kernel, count), out_shape=(shap...  20.1 us
    pallas_call x1, Pallas kernels, cross(): pl.pallas_call(functools.partial(cross_kernel, 1.0 / windows), grid=(loca...  18.1 us
    dot_general x1, matrix products, local(): jnp.einsum('cws,sj->wcj', samples, table, preferred_element_type=jnp.floa...  1.83 us
    unnamed x2, local copies, waits for them, and re-layouts  1.67 us

profile of v2, /device:TPU:0, one launch (start us, length us, event | category | flops | bytes accessed | tf_op | source)
XLA Modules:
  0.0 41.7 jit_solution(15202613387118478797)
XLA Ops:
  0.0 0.0 copy-start
  0.0 1.7 %copy-done = bf16[576,2,1024]{2,1,0:T(2,128)(2,1)S(1)} copy-done((bf16[576,2,1024]{2,1,0:T(2,128)(2,1)S(1)}, bf16[576,2,1024]{2,1,0:T(2,128)(2,1)}, u32[]{:S(2)}) %copy-start) | copy-done | bytes 2359320
  1.7 1.8 %fusion.5.spec_ref = bf16[2,576,256]{2,1,0:T(8,128)(2,1)S(1)} fusion(bf16[1024,256,1]{1,0,2:T(8,128)(2,1)} %constant.5, bf16[576,2,1024]{2,1,0:T(2,128)(2,1)S(1)} %copy-done), kind=kOutput, calls=%fused_computation.3 | convolution fusion | flops 604274688 | bytes 3473408 | tf_op jit(solution)/shard_map/cws,sj->wcj/dot_general | solution.py:225
  3.5 20.1 %exchange.1 = (bf16[16,16,1152]{2,1,0:T(8,128)(2,1)S(1)}, bf16[16,16,1152]{2,1,0:T(8,128)(2,1)S(1)}) custom-call(bf16[2,576,256]{2,1,0:T(8,128)(2,1)S(1)} %fusion.5.spec_ref), custom_call_target="tpu_custom_call" | custom-call | flops 5898240 | bytes 2359296 | tf_op jit(solution)/shard_map/exchange/pallas_call | solution.py:128
  23.6 18.1 %cross.1 = bf16[2,16,576,1152]{3,2,1,0:T(8,128)(2,1)} custom-call(bf16[16,16,1152]{2,1,0:T(8,128)(2,1)S(1)} %get-tuple-element.7.own_ref, bf16[16,16,1152]{2,1,0:T(8,128)(2,1)S(1)} %get-tuple-element.8.other_ref), custom_call_target="tpu_custom_call" | custom-call | flops 1358954496 | bytes 42467328 | tf_op jit(solution)/shard_map/cross/pallas_call | solution.py:202
Async XLA Ops:
  0.0 1.7 %copy-start = (bf16[576,2,1024]{2,1,0:T(2,128)(2,1)S(1)}, bf16[576,2,1024]{2,1,0:T(2,128)(2,1)}, u32[]{:S(2)}) copy-start(bf16[576,2,1024]{2,1,0:T(2,128)(2,1)} %param.2) | copy-start | bytes 7077892

commit v3 on v2

--- a/solution.py
+++ b/solution.py
@@ -68,15 +68,17 @@
         pl.semaphore_signal(barrier, inc=1, device_id=(hour, chan, peer), device_id_type=MESH)
     pl.semaphore_signal(barrier, inc=1, device_id=(hour, 1 - chan, me), device_id_type=MESH)
 
-    copies, keeps, passes = {}, [], []
-
-    def forward(source_ref, owner, w, step):
-        slot = w * count + step
+    copies, passes = {}, []
+
+    def block(owner):
+        return own_ref.at[pl.ds(windows * owner, windows)]
+
+    def forward(source_ref, owner, step):
         copy = pltpu.make_async_remote_copy(
             src_ref=source_ref,
-            dst_ref=other_ref.at[windows * owner + w],
-            send_sem=pass_sem.at[slot],
-            recv_sem=got_sem.at[slot],
+            dst_ref=other_ref.at[pl.ds(windows * owner, windows)],
+            send_sem=pass_sem.at[step],
+            recv_sem=got_sem.at[step],
             device_id=(hour, 1 - chan, me),
             device_id_type=MESH,
         )
@@ -84,36 +86,30 @@
         passes.append(copy)
 
     for w in range(windows):
-        turned = spec_ref[w].astype(jnp.float32).T
+        turned = spec_ref[w].T.astype(jnp.float32)
         real, imag = whiten(turned[:BINS], turned[BINS:])
         packed = pack(real, imag).astype(jnp.bfloat16)
-        white[w] = packed.reshape(count, local_bins, width)
-        if w == 0:
-            pl.semaphore_wait(barrier, count)
-        for step in steps:
-            peer = lax.rem(me + step, count)
-            copy = pltpu.make_async_remote_copy(
-                src_ref=white.at[w, peer],
-                dst_ref=own_ref.at[windows * me + w],
-                send_sem=send_sem.at[w * count + step],
-                recv_sem=recv_sem.at[w * count + step],
-                device_id=(hour, chan, peer),
-                device_id_type=MESH,
-            )
-            copy.start()
-            copies[w, step] = copy
-    for w in range(windows):
-        keep = pltpu.make_async_copy(white.at[w, me], own_ref.at[windows * me + w], local_sem.at[w])
-        keep.start()
-        keeps.append(keep)
-        forward(white.at[w, me], me, w, 0)
-    for w in range(windows):
-        for step in reversed(steps):
-            copies[w, step].wait_recv()
-            owner = lax.rem(me - step + count, count)
-            forward(own_ref.at[windows * owner + w], owner, w, step)
-    for keep in keeps:
-        keep.wait()
+        white[:, w] = packed.reshape(count, local_bins, width)
+    pl.semaphore_wait(barrier, count)
+    for step in steps:
+        peer = lax.rem(me + step, count)
+        copies[step] = pltpu.make_async_remote_copy(
+            src_ref=white.at[peer],
+            dst_ref=block(me),
+            send_sem=send_sem.at[step],
+            recv_sem=recv_sem.at[step],
+            device_id=(hour, chan, peer),
+            device_id_type=MESH,
+        )
+        copies[step].start()
+    keep = pltpu.make_async_copy(white.at[me], block(me), local_sem)
+    keep.start()
+    forward(white.at[me], me, 0)
+    for step in reversed(steps):
+        copies[step].wait_recv()
+        owner = lax.rem(me - step + count, count)
+        forward(block(owner), owner, step)
+    keep.wait()
     for copy in copies.values():
         copy.wait_send()
     for copy in passes:
@@ -124,17 +120,17 @@
     windows, channels, _ = spec.shape
     local_bins = BINS // count
     shape = jax.ShapeDtypeStruct((windows * count, local_bins, 2 * channels), jnp.bfloat16)
-    pieces = pltpu.SemaphoreType.DMA((windows * count,))
+    pieces = pltpu.SemaphoreType.DMA((count,))
     return pl.pallas_call(
         functools.partial(exchange_kernel, count),
         out_shape=(shape, shape),
         in_specs=[pl.BlockSpec(memory_space=pltpu.VMEM)],
         out_specs=(pl.BlockSpec(memory_space=pl.ANY), pl.BlockSpec(memory_space=pl.ANY)),
         scratch_shapes=[
-            pltpu.VMEM((windows, count, local_bins, 2 * channels), jnp.bfloat16),
-            pieces,
-            pieces,
-            pltpu.SemaphoreType.DMA((windows,)),
+            pltpu.VMEM((count, windows, local_bins, 2 * channels), jnp.bfloat16),
+            pieces,
+            pieces,
+            pltpu.SemaphoreType.DMA,
             pieces,
             pieces,
         ],

time: 41.9 us -> 41.3 us (0.986)
  the two profiles are of different devices: /device:TPU:0 before, /device:TPU:15 now
where the time goes in v3:
time: 41.3 us; the launch traced here: 41.1 us
  Pallas kernels  37.6 us (91%)
  matrix products  1.83 us (4%)
  local copies, waits for them, and re-layouts  1.67 us (4%)
    pallas_call x1, Pallas kernels, exchange(): pl.pallas_call(functools.partial(exchange_kernel, count), out_shape=(shap...  19.5 us
    pallas_call x1, Pallas kernels, cross(): pl.pallas_call(functools.partial(cross_kernel, 1.0 / windows), grid=(loca...  18.1 us
    dot_general x1, matrix products, local(): jnp.einsum('cws,sj->wcj', samples, table, preferred_element_type=jnp.floa...  1.83 us
    unnamed x2, local copies, waits for them, and re-layouts  1.67 us

profile of v3, /device:TPU:15, one launch (start us, length us, event | category | flops | bytes accessed | tf_op | source)
XLA Modules:
  0.0 41.1 jit_solution(10116348869412288941)
XLA Ops:
  0.0 0.0 copy-start
  0.0 1.7 %copy-done = bf16[576,2,1024]{2,1,0:T(2,128)(2,1)S(1)} copy-done((bf16[576,2,1024]{2,1,0:T(2,128)(2,1)S(1)}, bf16[576,2,1024]{2,1,0:T(2,128)(2,1)}, u32[]{:S(2)}) %copy-start) | copy-done | bytes 2359320
  1.7 1.8 %fusion.5.spec_ref = bf16[2,576,256]{2,1,0:T(8,128)(2,1)S(1)} fusion(bf16[1024,256,1]{1,0,2:T(8,128)(2,1)} %constant.5, bf16[576,2,1024]{2,1,0:T(2,128)(2,1)S(1)} %copy-done), kind=kOutput, calls=%fused_computation.3 | convolution fusion | flops 604274688 | bytes 3473408 | tf_op jit(solution)/shard_map/cws,sj->wcj/dot_general | solution.py:221
  3.5 19.5 %exchange.1 = (bf16[16,16,1152]{2,1,0:T(8,128)(2,1)S(1)}, bf16[16,16,1152]{2,1,0:T(8,128)(2,1)S(1)}) custom-call(bf16[2,576,256]{2,1,0:T(8,128)(2,1)S(1)} %fusion.5.spec_ref), custom_call_target="tpu_custom_call" | custom-call | flops 5898240 | bytes 2359296 | tf_op jit(solution)/shard_map/exchange/pallas_call | solution.py:124
  23.0 18.1 %cross.1 = bf16[2,16,576,1152]{3,2,1,0:T(8,128)(2,1)} custom-call(bf16[16,16,1152]{2,1,0:T(8,128)(2,1)S(1)} %get-tuple-element.7.own_ref, bf16[16,16,1152]{2,1,0:T(8,128)(2,1)S(1)} %get-tuple-element.8.other_ref), custom_call_target="tpu_custom_call" | custom-call | flops 1358954496 | bytes 42467328 | tf_op jit(solution)/shard_map/cross/pallas_call | solution.py:198
Async XLA Ops:
  0.0 1.7 %copy-start = (bf16[576,2,1024]{2,1,0:T(2,128)(2,1)S(1)}, bf16[576,2,1024]{2,1,0:T(2,128)(2,1)}, u32[]{:S(2)}) copy-start(bf16[576,2,1024]{2,1,0:T(2,128)(2,1)} %param.2) | copy-start | bytes 7077892
